TPU v7x, 512 devices: a whole 4x4x16 slice. The times are simulated.
512 devices in a mesh: rows: 128 (over y, z, core), grp: 4 (over x).
Axes of the slice: x: 4, y: 4, z: 16, core: 2. Of those that a mesh axis runs over, the one named last changes fastest.
Arguments:
- features: float32 [131072, 128], P(('rows', 'grp'))
- key_ids: int32 [131072], P(('rows', 'grp')), may hold values from 0 to 23, as said below
- owner: int32 [24], replicated, may hold values from 0 to 23, each once
Outputs:
- covariance: float32 [3072, 128], P(('rows', 'grp'))
Inputs may be any that keep to these rules, and one draw needn't show every extreme that they name: `key_ids`: every key is the key of at least 2 rows.
All inputs are finite; a program needn't handle non-finite values.
Results may differ from a plain program's by a relative error of at most 0.0003.
Values sent between devices are 32-bit elements; how exact they have to be, the bound alone decides.
No kernel may reach another device: no remote copies, remote signals or barrier semaphores. Data moves between devices by JAX's collectives and lax.ppermute only.
A program may use at most 64 MiB of HBM per device.

v0:
```python
import jax
import jax.numpy as jnp
from jax import lax
from jax.sharding import Mesh
from jax.sharding import PartitionSpec as P

ROWS = ("rows_0", "rows_1", "rows_2")
ROWS_GRP = ("rows_0", "rows_1", "rows_2", "grp")


def split_up(value, dim, size):
    before, after = (value.shape[:dim], value.shape[dim + 1 :])
    return jnp.moveaxis(value.reshape(*before, size, -1, *after), dim, 0)


def sum_at_owner(value, axis, dim):
    size = lax.axis_size(axis)
    tiles = lax.all_to_all(split_up(value, dim, size), axis, 0, 0, tiled=True)
    return jnp.sum(tiles, axis=0)


def summed_rows(value, axes, dim):
    far, near = axes
    own = sum_at_owner(split_up(value, dim, lax.axis_size(far)), near, dim + 1)
    return jnp.sum(lax.all_to_all(own, far, 0, 0, tiled=True), axis=0)


def local(features, key_ids, owner):
    nkeys = owner.shape[0]
    width = features.shape[1]
    labels = jnp.arange(nkeys, dtype=jnp.int32)
    member = key_ids[:, None] == labels[None, :]
    slot = jnp.sum(jnp.where(member, owner[None, :], 0), axis=1)
    onehot = (slot[:, None] == labels[None, :]).astype(jnp.float32)
    contract = (((0,), (0,)), ((), ()))
    local_total = lax.dot_general(
        onehot,
        features,
        contract,
        precision=lax.Precision.HIGHEST,
        preferred_element_type=jnp.float32,
    )
    local_count = jnp.sum(onehot, axis=0)
    weighted = (onehot[:, :, None] * features[:, None, :]).reshape(features.shape[0], nkeys * width)
    gram_flat = lax.dot_general(
        weighted,
        features,
        contract,
        precision=lax.Precision.HIGHEST,
        preferred_element_type=jnp.float32,
    )
    n_rows = lax.axis_size(ROWS)
    n_grp = lax.axis_size("grp")
    local_rows = nkeys * width // (n_rows * n_grp)
    extra = local_rows // width + 2
    block_rows = local_rows + extra + 1
    count_line = jnp.zeros((1, width), jnp.float32).at[0, :nkeys].set(local_count)
    source = jnp.concatenate(
        [gram_flat, local_total, count_line, jnp.zeros((1, width), jnp.float32)], axis=0
    )
    count_index = nkeys * width + nkeys
    zero_index = count_index + 1
    index = jnp.arange(block_rows * lax.axis_size(ROWS_GRP), dtype=jnp.int32)
    device = index // block_rows
    within = index % block_rows
    base = device * local_rows
    first_key = base // width
    sum_key = first_key + within - local_rows
    sum_index = jnp.where(sum_key < nkeys, nkeys * width + sum_key, zero_index)
    chosen = jnp.where(
        within < local_rows,
        base + within,
        jnp.where(within < local_rows + extra, sum_index, count_index),
    )
    received = summed_rows(
        jnp.take(source, chosen, axis=0), (("rows_0", "rows_1"), ("rows_2", "grp")), 0
    )
    position = lax.axis_index(ROWS) * n_grp + lax.axis_index("grp")
    base = position * local_rows
    target = base + jnp.arange(local_rows, dtype=jnp.int32)
    owner_slot = target // width
    column = target % width
    gram = received[:local_rows]
    sums = received[local_rows : local_rows + extra]
    counts = received[local_rows + extra]
    slot_total = jnp.take(sums, owner_slot - base // width, axis=0)
    slot_count = jnp.take(counts, owner_slot, axis=0)[:, None]
    own_total = jnp.take_along_axis(slot_total, column[:, None], axis=1)
    centred = gram - own_total * slot_total / slot_count
    return centred / (slot_count - 1.0)


def solution(mesh):
    torus = Mesh(
        mesh.devices.reshape(4, 16, 2, mesh.shape["grp"]), ("rows_0", "rows_1", "rows_2", "grp")
    )
    in_specs = (P(ROWS_GRP, None), P(ROWS_GRP), P())
    out_specs = P(ROWS_GRP, None)
    return jax.shard_map(local, mesh=torus, in_specs=in_specs, out_specs=out_specs, check_vma=False)
```

profile of v0, /device:TPU:24, one launch (start us, length us, event | category | flops | bytes accessed | tf_op | source)
XLA Modules:
  0.0 118.0 jit_solution(14962416661551956329)
XLA Ops:
  0.0 0.0 copy-start
  0.0 0.8 select_reduce_fusion
  0.8 0.1 fusion.17
  0.9 0.6 compare_reduce_fusion
  1.6 0.3 fusion.14
  1.9 0.6 compare_and_fusion
  2.4 0.1 copy.8
  2.5 1.1 fusion.12
  3.6 1.8 %broadcast_multiply_fusion = f32[256,24,128]{2,1,0:T(8,128)S(1)} fusion(f32[256,128]{1,0:T(8,128)} %param.5, f32[256,24]{1,0:T(8,128)S(1)} %copy.8), kind=kLoop, calls=%fused_computation.8 | loop fusion | flops 786432 | bytes 3301376 | tf_op jit(solution)/shard_map/mul | solution.py:44
  5.4 0.0 copy-done
  5.4 5.1 %fusion = f32[3072,128]{1,0:T(8,128)S(1)} fusion(f32[256,128]{1,0:T(8,128)S(1)} %copy-done, f32[32,8,24,128]{3,2,1,0:T(8,128)S(1)} %bitcast.20), kind=kOutput, calls=%fused_computation.5 | convolution fusion | flops 1207959552 | bytes 4849664 | tf_op jit(solution)/shard_map/dot_general | solution.py:45
  10.5 0.7 fusion.19
  11.2 0.3 concatenate.5
  11.5 9.3 %gather_fusion = f32[4608,128]{1,0:T(8,128)} fusion(f32[3098,128]{1,0:T(8,128)S(1)} %concatenate.5, s32[5120]{0:T(1024)S(1)} %pad_clamp_fusion), kind=kCustom, calls=%fused_computation | custom fusion | bytes 4737024 | tf_op jit(solution)/shard_map/jit(_take)/gather | solution.py:76
  20.8 4.2 %gather.21 = f32[64,8,9,128]{3,2,1,0:T(8,128)} reshape(f32[4608,128]{1,0:T(8,128)} %gather_fusion) | data formatting | bytes 4718592 | tf_op jit(solution)/shard_map/jit(_take)/gather | solution.py:76
  25.0 3.6 %select_bitcast_fusion = f32[8,64,9,128]{3,2,0,1:T(8,128)S(1)} fusion(f32[64,8,9,128]{3,2,1,0:T(8,128)} %gather.21, pred[64,8,9]{2,1,0:T(8,128)(4,1)S(1)} %compare_and_fusion), kind=kLoop, calls=%fused_computation.4 | loop fusion | flops 589824 | bytes 4723200 | tf_op jit(solution)/shard_map/transpose | solution.py:13
  28.5 1.4 %copy.9 = f32[8,64,9,128]{3,1,2,0:T(8,128)S(1)} copy(f32[8,64,9,128]{3,2,0,1:T(8,128)S(1)} %select_bitcast_fusion) | data formatting | bytes 4718592 | tf_op jit(solution)/shard_map/transpose | solution.py:13
  29.9 33.5 %all_to_all.10 = f32[8,64,9,128]{3,1,2,0:T(8,128)S(1)} all-to-all(f32[8,64,9,128]{3,1,2,0:T(8,128)S(1)} %copy.9), channel_id=1, replica_groups=mesh['rows_0'=4,'rows_1'=16,'rows_2'=2,'grp'=4] {'rows_2','grp'}, dimensions={0} | all-to-all | bytes 4718592 | tf_op jit(solution)/shard_map/all_to_all | solution.py:18
  63.4 0.2 reduce_sum.38
  63.6 1.0 copy.10
  64.5 18.7 %all-to-all-start.1 = ((f32[64,9,128]{2,1,0:T(8,128)}), f32[64,9,128]{2,1,0:T(8,128)S(1)}, u32[]{:S(2)}, u32[]{:S(2)}) async-start(f32[64,9,128]{2,1,0:T(8,128)} %copy.10), calls=%async_computation.1 | async-start | bytes 1048576 | tf_op jit(solution)/shard_map/all_to_all | solution.py:25
  83.4 31.8 %all-to-all-done.1 = f32[64,9,128]{2,1,0:T(8,128)S(1)} async-done(((f32[64,9,128]{2,1,0:T(8,128)}), f32[64,9,128]{2,1,0:T(8,128)S(1)}, u32[]{:S(2)}, u32[]{:S(2)}) %all-to-all-start.1) | async-done | bytes 294944 | tf_op jit(solution)/shard_map/all_to_all | solution.py:25
  115.2 0.1 reduce_sum.39
  115.3 0.6 gather_fusion.2
  116.0 0.6 gather_fusion.1
  116.5 0.1 broadcast_select_fusion
  116.6 0.6 gather_fusion.3
  117.3 0.7 fusion.18
  (16 shorter events, 0.1 us)
Async XLA Ops:
  0.0 5.4 %copy-start = (f32[256,128]{1,0:T(8,128)S(1)}, f32[256,128]{1,0:T(8,128)}, u32[]{:S(2)}) copy-start(f32[256,128]{1,0:T(8,128)} %param.5) | copy-start | bytes 393220
  64.5 50.7 %all-to-all-start.1 = ((f32[64,9,128]{2,1,0:T(8,128)}), f32[64,9,128]{2,1,0:T(8,128)S(1)}, u32[]{:S(2)}, u32[]{:S(2)}) async-start(f32[64,9,128]{2,1,0:T(8,128)} %copy.10), calls=%async_computation.1 | async-start | bytes 1048576 | tf_op jit(solution)/shard_map/all_to_all | solution.py:25
where the time goes:
time: 118 us
  blocking collectives  33.5 us (28%)
  waiting for transfers between devices  31.8 us (27%)
  starting transfers between devices  18.7 us (16%)
  local copies, waits for them, and re-layouts  18.1 us (15%)
  other arithmetic  9.53 us (8%)
  matrix products  6.14 us (5%)
    all_to_all x1, blocking collectives, sum_at_owner(): tiles = lax.all_to_all(split_up(value, dim, size), axis, 0, 0, tiled=True)  33.5 us
    all_to_all x1, waiting for transfers between devices, summed_rows(): return jnp.sum(lax.all_to_all(own, far, 0, 0, tiled=True), axis=0)  31.8 us
    all_to_all x1, starting transfers between devices, summed_rows(): return jnp.sum(lax.all_to_all(own, far, 0, 0, tiled=True), axis=0)  18.7 us
    gather x2, local copies, waits for them, and re-layouts, local(): jnp.take(source, chosen, axis=0)  13.4 us
    dot_general x1, matrix products, local(): lax.dot_general(weighted, features, contract, precision=lax.Precision.HIG...  5.08 us
    transpose x1, other arithmetic, split_up(): return jnp.moveaxis(value.reshape(*before, size, -1, *after), dim, 0)  3.57 us
  transfers between devices with their start and end apart: 1, of which 1 were waited for; matrix products, arithmetic and copies ran while one was open for 0% of the time, Pallas kernels for 0%

commit v1 on v0

v1 whole, which is shorter than its diff:
```python
import jax
import jax.numpy as jnp
from jax import lax
from jax.experimental import pallas as pl
from jax.experimental.pallas import tpu as pltpu
from jax.sharding import Mesh
from jax.sharding import PartitionSpec as P

Y, Z, C, X = "y", "z", "c", "x"
ALL = (Y, Z, C, X)
F = 128
KEYS = 24
NY, NZ, NX = 4, 16, 4
OWN = 6
PACK = 264
MSG = 104
VMEM = pl.BlockSpec(memory_space=pltpu.VMEM)
SMEM = pl.BlockSpec(memory_space=pltpu.SMEM)
PARAMS = pltpu.CompilerParams(vmem_limit_bytes=16 * 1024 * 1024)


def pack_kernel(owner_ref, features_ref, keys_ref, out_ref):
    keys = keys_ref[...]
    slot = jnp.zeros(keys.shape, jnp.float32)
    for key in range(KEYS):
        slot = jnp.where(keys == key, owner_ref[key].astype(jnp.float32), slot)
    rows = features_ref.shape[0]
    out_ref[0:rows, :] = features_ref[...]
    out_ref[rows:, :] = jnp.concatenate([slot, jnp.zeros((6, F), jnp.float32)], axis=0)


def gram_kernel(rows_ref, out_ref):
    c = lax.axis_index(C)
    rows = PACK - 8
    feats = jnp.concatenate([rows_ref[0:rows, :], rows_ref[PACK : PACK + rows, :]], axis=0)
    first, second = rows_ref[rows:PACK, :], rows_ref[PACK + rows :, :]
    slot = jnp.concatenate([first[0:1], first[1:2], second[0:1], second[1:2]], axis=1)
    hi = feats.astype(jnp.bfloat16)
    lo = (feats - hi.astype(jnp.float32)).astype(jnp.bfloat16)
    both = jnp.concatenate([hi, lo], axis=1)

    m = NX * OWN * 8
    index = lax.broadcasted_iota(jnp.int32, (m, 1), 0)
    line = 48 * (index & 7) + 24 * c + (index >> 3)
    lane = lax.broadcasted_iota(jnp.int32, (m, F), 1)
    select = (lane == (line & 127)).astype(jnp.float32).astype(jnp.bfloat16)
    nt = (((1,), (1,)), ((), ()))
    nn = (((1,), (0,)), ((), ()))
    left_hi = lax.dot_general(select, hi, nt, preferred_element_type=jnp.float32)
    left_lo = lax.dot_general(select, lo, nt, preferred_element_type=jnp.float32)
    relative = slot - (line >> 7).astype(jnp.float32)

    index = lax.broadcasted_iota(jnp.int32, (32, 1), 0)
    wanted = jnp.where((index & 7) < 6, 6 * (index >> 3) + (index & 7), -1).astype(jnp.float32)
    onehot = (slot == wanted).astype(jnp.float32).astype(jnp.bfloat16)
    total = lax.dot_general(onehot, both, nn, preferred_element_type=jnp.float32)
    total = total[:, :F] + total[:, F:]
    label = lax.broadcasted_iota(jnp.int32, (F, 1), 0).astype(jnp.float32)
    every = (slot == label).astype(jnp.float32).astype(jnp.bfloat16)
    ones = jnp.ones((16, slot.shape[1]), jnp.bfloat16)
    count = lax.dot_general(ones, every, nt, preferred_element_type=jnp.float32)[0:8]
    sub = lax.broadcasted_iota(jnp.int32, (8, F), 0)
    for y in range(NY):
        tile = jnp.where(sub < 6, total[8 * y : 8 * y + 8], count)
        for x in range(NX):
            out_ref[y * NX + x, 96:104, :] = tile

    for group in range(8):
        y, half = group // 2, group % 2
        mine = relative == float(3 * group)
        a = jnp.where(mine, left_hi, 0.0).astype(jnp.bfloat16)
        b = jnp.where(mine, left_lo, 0.0).astype(jnp.bfloat16)
        wide = lax.dot_general(a, both, nn, preferred_element_type=jnp.float32)
        gram = wide[:, :F] + (
            wide[:, F:] + lax.dot_general(b, hi, nn, preferred_element_type=jnp.float32)
        )
        for x in range(NX):
            for i in range(OWN):
                at = (x * OWN + i) * 8
                out_ref[y * NX + x, i * 16 + half * 8 : i * 16 + half * 8 + 8, :] = gram[at : at + 8]


def relay_kernel(in_ref, out_ref):
    y, c, x = lax.axis_index(Y), lax.axis_index(C), lax.axis_index(X)
    total = jnp.sum(in_ref[...], axis=0)
    sums, counts = total[96:104], total[102:103]
    z = lax.broadcasted_iota(jnp.int32, (NZ, 1), 0)
    lane = lax.broadcasted_iota(jnp.int32, (NZ, F), 1)
    line = 48 * z + 24 * c + 6 * x
    head, tail = line >> 7, (line + 5) >> 7

    def pick(which):
        out = jnp.zeros((NZ, F), jnp.float32)
        for j in range(6):
            out = jnp.where(which == j, sums[j : j + 1], out)
        return out

    def number(which):
        return jnp.sum(jnp.where(lane == which + 6 * y, counts, 0.0), axis=1, keepdims=True)

    for i in range(OWN):
        part = total[16 * i : 16 * i + 16]
        if i == 1:
            part = jnp.where(lane == (line & 127), number(head), part)
        if i == 5:
            part = jnp.where(lane == ((line + 4) & 127), number(tail), part)
        out_ref[:, i, :] = part
    out_ref[:, 6, :] = pick(head)
    out_ref[:, 7, :] = pick(tail)


def final_kernel(in_ref, out_ref):
    z, c, x = lax.axis_index(Z), lax.axis_index(C), lax.axis_index(X)
    total = jnp.sum(in_ref[...], axis=0)
    start = (48 * z + 24 * c + 6 * x) & 127
    lane = lax.broadcasted_iota(jnp.int32, (1, F), 1)

    def entry(row, column):
        return jnp.sum(jnp.where(lane == column, total[row : row + 1], 0.0), axis=1, keepdims=True)

    fifth = (start + 4) & 127
    count_head, count_tail = entry(1, start), entry(5, fifth)
    fix_head, fix_tail = entry(0, start + 1), entry(4, fifth + 1)
    sub = lax.broadcasted_iota(jnp.int32, (8, 1), 0)
    wide = lax.broadcasted_iota(jnp.int32, (8, F), 1)
    gram = jnp.where((sub == 1) & (wide == start), fix_head, total)
    gram = jnp.where((sub == 5) & (wide == fifth), fix_tail, gram)
    in_head = start + sub < F
    slot_total = jnp.where(in_head, total[6:7], total[7:8])
    count = jnp.where(in_head, count_head, count_tail)
    own = jnp.sum(jnp.where(wide == ((start + sub) & 127), slot_total, 0.0), axis=1, keepdims=True)
    result = (gram - own * slot_total / count) / (count - 1.0)
    out_ref[...] = result[0:OWN]


def local(features, key_ids, owner):
    packed = pl.pallas_call(
        pack_kernel,
        out_shape=jax.ShapeDtypeStruct((PACK, F), jnp.float32),
        in_specs=[SMEM, VMEM, VMEM],
        out_specs=VMEM,
        compiler_params=PARAMS,
        name="pack",
    )(owner, features, key_ids.reshape(2, F))
    pair = lax.all_gather(packed, C, tiled=True)
    partial = pl.pallas_call(
        gram_kernel,
        out_shape=jax.ShapeDtypeStruct((NY * NX, MSG, F), jnp.float32),
        in_specs=[VMEM],
        out_specs=VMEM,
        compiler_params=PARAMS,
        name="gram",
    )(pair)
    near = lax.all_to_all(partial, (Y, X), 0, 0, tiled=True)
    relayed = pl.pallas_call(
        relay_kernel,
        out_shape=jax.ShapeDtypeStruct((NZ, 8, F), jnp.float32),
        in_specs=[VMEM],
        out_specs=VMEM,
        compiler_params=PARAMS,
        name="relay",
    )(near)
    far = lax.all_to_all(relayed, Z, 0, 0, tiled=True)
    return pl.pallas_call(
        final_kernel,
        out_shape=jax.ShapeDtypeStruct((OWN, F), jnp.float32),
        in_specs=[VMEM],
        out_specs=VMEM,
        compiler_params=PARAMS,
        name="finish",
    )(far)


def solution(mesh):
    torus = Mesh(mesh.devices.reshape(NY, NZ, 2, NX), ALL)
    in_specs = (P(ALL, None), P(ALL), P())
    return jax.shard_map(local, mesh=torus, in_specs=in_specs, out_specs=P(ALL, None), check_vma=False)
```

time: 118 us -> 55.4 us (0.47)
  the two profiles are of different devices: /device:TPU:24 before, /device:TPU:2 now
where the time goes in v1:
time: 55.4 us; the launch traced here: 55.2 us
  blocking collectives  51.1 us (92%)
  Pallas kernels  2.55 us (5%)
  local copies, waits for them, and re-layouts  1.6 us (3%)
    all_to_all x1, blocking collectives, local(): far = lax.all_to_all(relayed, Z, 0, 0, tiled=True)  26.4 us
    all_to_all x1, blocking collectives, local(): near = lax.all_to_all(partial, (Y, X), 0, 0, tiled=True)  22.7 us
    all_gather x1, blocking collectives, local(): pair = lax.all_gather(packed, C, tiled=True)  2 us
    unnamed x6, local copies, waits for them, and re-layouts  1.6 us
    pallas_call x1, Pallas kernels, local(): pl.pallas_call(gram_kernel, out_shape=jax.ShapeDtypeStruct((NY * NX, MSG,...  1.19 us

profile of v1, /device:TPU:2, one launch (start us, length us, event | category | flops | bytes accessed | tf_op | source)
XLA Modules:
  0.0 55.2 jit_solution(16278109192954671100)
XLA Ops:
  0.0 0.0 copy-start.2
  0.0 0.0 copy-start.1
  0.0 0.7 %copy-done.2 = s32[24]{0:T(128)S(1)} copy-done((s32[24]{0:T(128)S(1)}, s32[24]{0:T(128)}, u32[]{:S(2)}) %copy-start.2) | copy-done | bytes 120
  0.7 0.0 copy-done.1
  0.7 0.0 copy-start
  0.7 0.9 %copy-done = f32[256,128]{1,0:T(8,128)S(1)} copy-done((f32[256,128]{1,0:T(8,128)S(1)}, f32[256,128]{1,0:T(8,128)}, u32[]{:S(2)}) %copy-start) | copy-done | bytes 131096
  1.6 0.6 %pack.1 = f32[264,128]{1,0:T(8,128)S(1)} custom-call(s32[24]{0:T(128)S(1)} %copy-done.2, f32[256,128]{1,0:T(8,128)S(1)} %copy-done, s32[2,128]{1,0:T(2,128)S(1)} %bitcast.1), custom_call_target="tpu_custom_call" | custom-call | tf_op jit(solution)/shard_map/pack/pallas_call | solution.py:137
  2.2 2.0 %all_gather.3.rows_ref = f32[528,128]{1,0:T(8,128)S(1)} all-gather(f32[264,128]{1,0:T(8,128)S(1)} %pack.1), channel_id=1, replica_groups=mesh['y'=4,'z'=16,'c'=2,'x'=4] {'c'}, dimensions={0}, use_global_device_ids=true | all-gather | bytes 405504 | tf_op jit(solution)/shard_map/all_gather | solution.py:145
  4.2 1.2 %gram.1 = f32[16,104,128]{2,1,0:T(8,128)S(1)} custom-call(f32[528,128]{1,0:T(8,128)S(1)} %all_gather.3.rows_ref), custom_call_target="tpu_custom_call" | custom-call | tf_op jit(solution)/shard_map/gram/pallas_call | solution.py:146
  5.4 22.7 %all_to_all.10.in_ref = f32[16,104,128]{2,1,0:T(8,128)S(1)} all-to-all(f32[16,104,128]{2,1,0:T(8,128)S(1)} %gram.1), channel_id=1, replica_groups=mesh['y'=4,'z'=16,'c'=2,'x'=4] {'y','x'}, dimensions={0} | all-to-all | bytes 1703936 | tf_op jit(solution)/shard_map/all_to_all | solution.py:154
  28.1 0.1 relay.1
  28.2 26.4 %all_to_all.11.in_ref = f32[16,8,128]{2,1,0:T(8,128)S(1)} all-to-all(f32[16,8,128]{2,1,0:T(8,128)S(1)} %relay.1), channel_id=1, replica_groups=mesh['y'=4,'z'=16,'c'=2,'x'=4] {'z'}, dimensions={0} | all-to-all | bytes 131072 | tf_op jit(solution)/shard_map/all_to_all | solution.py:163
  54.5 0.7 %finish.1 = f32[6,128]{1,0:T(8,128)} custom-call(f32[16,8,128]{2,1,0:T(8,128)S(1)} %all_to_all.11.in_ref), custom_call_target="tpu_custom_call" | custom-call | tf_op jit(solution)/shard_map/finish/pallas_call | solution.py:164
Async XLA Ops:
  0.0 0.7 %copy-start.2 = (s32[24]{0:T(128)S(1)}, s32[24]{0:T(128)}, u32[]{:S(2)}) copy-start(s32[24]{0:T(128)} %owner_ref.1) | copy-start | bytes 292
  0.0 0.7 %copy-start.1 = (s32[256]{0:T(256)S(1)}, s32[256]{0:T(256)}, u32[]{:S(2)}) copy-start(s32[256]{0:T(256)} %param.4) | copy-start | bytes 3076
  0.7 0.9 %copy-start = (f32[256,128]{1,0:T(8,128)S(1)}, f32[256,128]{1,0:T(8,128)}, u32[]{:S(2)}) copy-start(f32[256,128]{1,0:T(8,128)} %features_ref.1) | copy-start | bytes 393220

commit v2 on v1

--- a/solution.py
+++ b/solution.py
@@ -15,18 +15,30 @@
 PACK = 264
 MSG = 104
 VMEM = pl.BlockSpec(memory_space=pltpu.VMEM)
-SMEM = pl.BlockSpec(memory_space=pltpu.SMEM)
+HBM = pl.BlockSpec(memory_space=pltpu.HBM)
+Y0, Z0, X0 = 2, 10, 2
+NEAR = [(i + X0) % NX * NY + (j + Y0) % NY for i in range(NX) for j in range(NY)]
+FAR = [(k + Z0) % NZ for k in range(NZ)]
 PARAMS = pltpu.CompilerParams(vmem_limit_bytes=16 * 1024 * 1024)
 
 
-def pack_kernel(owner_ref, features_ref, keys_ref, out_ref):
-    keys = keys_ref[...]
+def pack_kernel(owner_ref, features_ref, keys_ref, out_ref, owner_buf, keys_buf, sems):
+    rows = features_ref.shape[0]
+    copies = [
+        pltpu.make_async_copy(owner_ref, owner_buf, sems.at[0]),
+        pltpu.make_async_copy(keys_ref, keys_buf, sems.at[1]),
+        pltpu.make_async_copy(features_ref, out_ref.at[0:rows, :], sems.at[2]),
+    ]
+    for copy in copies:
+        copy.start()
+    copies[0].wait()
+    copies[1].wait()
+    keys = keys_buf[...]
     slot = jnp.zeros(keys.shape, jnp.float32)
     for key in range(KEYS):
-        slot = jnp.where(keys == key, owner_ref[key].astype(jnp.float32), slot)
-    rows = features_ref.shape[0]
-    out_ref[0:rows, :] = features_ref[...]
+        slot = jnp.where(keys == key, owner_buf[key].astype(jnp.float32), slot)
     out_ref[rows:, :] = jnp.concatenate([slot, jnp.zeros((6, F), jnp.float32)], axis=0)
+    copies[2].wait()
 
 
 def gram_kernel(rows_ref, out_ref):
@@ -63,7 +75,7 @@
     for y in range(NY):
         tile = jnp.where(sub < 6, total[8 * y : 8 * y + 8], count)
         for x in range(NX):
-            out_ref[y * NX + x, 96:104, :] = tile
+            out_ref[NEAR.index(x * NY + y), 96:104, :] = tile
 
     for group in range(8):
         y, half = group // 2, group % 2
@@ -77,7 +89,7 @@
         for x in range(NX):
             for i in range(OWN):
                 at = (x * OWN + i) * 8
-                out_ref[y * NX + x, i * 16 + half * 8 : i * 16 + half * 8 + 8, :] = gram[at : at + 8]
+                out_ref[NEAR.index(x * NY + y), i * 16 + half * 8 : i * 16 + half * 8 + 8, :] = gram[at : at + 8]
 
 
 def relay_kernel(in_ref, out_ref):
@@ -98,15 +110,19 @@
     def number(which):
         return jnp.sum(jnp.where(lane == which + 6 * y, counts, 0.0), axis=1, keepdims=True)
 
+    def put(i, part):
+        out_ref[0 : NZ - Z0, i, :] = part[Z0:]
+        out_ref[NZ - Z0 :, i, :] = part[:Z0]
+
     for i in range(OWN):
         part = total[16 * i : 16 * i + 16]
         if i == 1:
             part = jnp.where(lane == (line & 127), number(head), part)
         if i == 5:
             part = jnp.where(lane == ((line + 4) & 127), number(tail), part)
-        out_ref[:, i, :] = part
-    out_ref[:, 6, :] = pick(head)
-    out_ref[:, 7, :] = pick(tail)
+        put(i, part)
+    put(6, pick(head))
+    put(7, pick(tail))
 
 
 def final_kernel(in_ref, out_ref):
@@ -137,11 +153,16 @@
     packed = pl.pallas_call(
         pack_kernel,
         out_shape=jax.ShapeDtypeStruct((PACK, F), jnp.float32),
-        in_specs=[SMEM, VMEM, VMEM],
+        in_specs=[HBM, HBM, HBM],
         out_specs=VMEM,
+        scratch_shapes=[
+            pltpu.SMEM((KEYS,), jnp.int32),
+            pltpu.VMEM((2, F), jnp.int32),
+            pltpu.SemaphoreType.DMA((3,)),
+        ],
         compiler_params=PARAMS,
         name="pack",
-    )(owner, features, key_ids.reshape(2, F))
+    )(*(pltpu.with_memory_space_constraint(v, pltpu.HBM) for v in (owner, features, key_ids.reshape(2, F))))
     pair = lax.all_gather(packed, C, tiled=True)
     partial = pl.pallas_call(
         gram_kernel,
@@ -151,7 +172,7 @@
         compiler_params=PARAMS,
         name="gram",
     )(pair)
-    near = lax.all_to_all(partial, (Y, X), 0, 0, tiled=True)
+    near = lax.all_to_all(partial, (X, Y), 0, 0, axis_index_groups=[NEAR], tiled=True)
     relayed = pl.pallas_call(
         relay_kernel,
         out_shape=jax.ShapeDtypeStruct((NZ, 8, F), jnp.float32),
@@ -160,7 +181,7 @@
         compiler_params=PARAMS,
         name="relay",
     )(near)
-    far = lax.all_to_all(relayed, Z, 0, 0, tiled=True)
+    far = lax.all_to_all(relayed, Z, 0, 0, axis_index_groups=[FAR], tiled=True)
     return pl.pallas_call(
         final_kernel,
         out_shape=jax.ShapeDtypeStruct((OWN, F), jnp.float32),

time: 55.4 us -> 46.5 us (0.84)
  the two profiles are of different devices: /device:TPU:2 before, /device:TPU:24 now
where the time goes in v2:
time: 46.5 us; the launch traced here: 45.6 us
  blocking collectives  42.7 us (92%)
  Pallas kernels  2.94 us (6%)
    all_to_all x1, blocking collectives, local(): lax.all_to_all(partial, (X, Y), 0, 0, axis_index_groups=[NEAR], tiled=True)  22.1 us
    all_to_all x1, blocking collectives, local(): far = lax.all_to_all(relayed, Z, 0, 0, axis_index_groups=[FAR], tiled=True)  18.6 us
    all_gather x1, blocking collectives, local(): pair = lax.all_gather(packed, C, tiled=True)  2 us
    pallas_call x1, Pallas kernels, local(): pl.pallas_call(gram_kernel, out_shape=jax.ShapeDtypeStruct((NY * NX, MSG,...  1.19 us
    pallas_call x1, Pallas kernels, local(): pl.pallas_call(pack_kernel, out_shape=jax.ShapeDtypeStruct((PACK, F), jnp...  0.95 us

profile of v2, /device:TPU:24, one launch (start us, length us, event | category | flops | bytes accessed | tf_op | source)
XLA Modules:
  0.0 45.6 jit_solution(17318085316950255371)
XLA Ops:
  0.0 0.9 %pack.1 = f32[264,128]{1,0:T(8,128)S(1)} custom-call(s32[24]{0:T(128)} %owner_ref.1, f32[256,128]{1,0:T(8,128)} %features_ref.1, s32[2,128]{1,0:T(2,128)} %bitcast.1), custom_call_target="tpu_custom_call" | custom-call | tf_op jit(solution)/shard_map/pack/pallas_call | solution.py:153
  1.0 2.0 %all_gather.3.rows_ref = f32[528,128]{1,0:T(8,128)S(1)} all-gather(f32[264,128]{1,0:T(8,128)S(1)} %pack.1), channel_id=1, replica_groups=mesh['y'=4,'z'=16,'c'=2,'x'=4] {'c'}, dimensions={0}, use_global_device_ids=true | all-gather | bytes 405504 | tf_op jit(solution)/shard_map/all_gather | solution.py:166
  3.0 1.2 %gram.1 = f32[16,104,128]{2,1,0:T(8,128)S(1)} custom-call(f32[528,128]{1,0:T(8,128)S(1)} %all_gather.3.rows_ref), custom_call_target="tpu_custom_call" | custom-call | tf_op jit(solution)/shard_map/gram/pallas_call | solution.py:167
  4.1 22.1 %all_to_all.10.in_ref = f32[16,104,128]{2,1,0:T(8,128)S(1)} all-to-all(f32[16,104,128]{2,1,0:T(8,128)S(1)} %gram.1), channel_id=1, replica_groups={{258,386,2,130,259,387,3,131,256,384,0,128,257,385,1,129},{262,390,6,13..., dimensions={0} | all-to-all | bytes 1703936 | tf_op jit(solution)/shard_map/all_to_all | solution.py:175
  26.2 0.1 relay.1
  26.3 18.6 %all_to_all.11.in_ref = f32[16,8,128]{2,1,0:T(8,128)S(1)} all-to-all(f32[16,8,128]{2,1,0:T(8,128)S(1)} %relay.1), channel_id=1, replica_groups={{80,88,96,104,112,120,0,8,16,24,32,40,48,56,64,72},{81,89,97,105,113,12..., dimensions={0} | all-to-all | bytes 131072 | tf_op jit(solution)/shard_map/all_to_all | solution.py:184
  44.9 0.7 %finish.1 = f32[6,128]{1,0:T(8,128)} custom-call(f32[16,8,128]{2,1,0:T(8,128)S(1)} %all_to_all.11.in_ref), custom_call_target="tpu_custom_call" | custom-call | tf_op jit(solution)/shard_map/finish/pallas_call | solution.py:185

commit v3 on v2

--- a/solution.py
+++ b/solution.py
@@ -13,12 +13,13 @@
 NY, NZ, NX = 4, 16, 4
 OWN = 6
 PACK = 264
-MSG = 104
+MSG = 56
 VMEM = pl.BlockSpec(memory_space=pltpu.VMEM)
 HBM = pl.BlockSpec(memory_space=pltpu.HBM)
-Y0, Z0, X0 = 2, 10, 2
+Y0, Z0, X0 = 2, 5, 2
 NEAR = [(i + X0) % NX * NY + (j + Y0) % NY for i in range(NX) for j in range(NY)]
-FAR = [(k + Z0) % NZ for k in range(NZ)]
+FAR = [[(2 * (k + Z0) + odd) % NZ for k in range(8)] for odd in range(2)]
+PAIRS = [[4 * k + j for j in range(4)] for k in range(8)]
 PARAMS = pltpu.CompilerParams(vmem_limit_bytes=16 * 1024 * 1024)
 
 
@@ -42,18 +43,19 @@
 
 
 def gram_kernel(rows_ref, out_ref):
-    c = lax.axis_index(C)
+    c, z = lax.axis_index(C), lax.axis_index(Z)
     rows = PACK - 8
-    feats = jnp.concatenate([rows_ref[0:rows, :], rows_ref[PACK : PACK + rows, :]], axis=0)
-    first, second = rows_ref[rows:PACK, :], rows_ref[PACK + rows :, :]
-    slot = jnp.concatenate([first[0:1], first[1:2], second[0:1], second[1:2]], axis=1)
+    starts = range(0, 4 * PACK, PACK)
+    feats = jnp.concatenate([rows_ref[at : at + rows, :] for at in starts], axis=0)
+    slots = [rows_ref[at + rows : at + PACK, :] for at in starts]
+    slot = jnp.concatenate([s[j : j + 1] for s in slots for j in range(2)], axis=1)
     hi = feats.astype(jnp.bfloat16)
     lo = (feats - hi.astype(jnp.float32)).astype(jnp.bfloat16)
     both = jnp.concatenate([hi, lo], axis=1)
 
     m = NX * OWN * 8
     index = lax.broadcasted_iota(jnp.int32, (m, 1), 0)
-    line = 48 * (index & 7) + 24 * c + (index >> 3)
+    line = 96 * (index & 7) + 48 * (z & 1) + 24 * c + (index >> 3)
     lane = lax.broadcasted_iota(jnp.int32, (m, F), 1)
     select = (lane == (line & 127)).astype(jnp.float32).astype(jnp.bfloat16)
     nt = (((1,), (1,)), ((), ()))
@@ -73,36 +75,33 @@
     count = lax.dot_general(ones, every, nt, preferred_element_type=jnp.float32)[0:8]
     sub = lax.broadcasted_iota(jnp.int32, (8, F), 0)
     for y in range(NY):
-        tile = jnp.where(sub < 6, total[8 * y : 8 * y + 8], count)
-        for x in range(NX):
-            out_ref[NEAR.index(x * NY + y), 96:104, :] = tile
-
-    for group in range(8):
-        y, half = group // 2, group % 2
-        mine = relative == float(3 * group)
+        mine = relative == float(6 * y)
         a = jnp.where(mine, left_hi, 0.0).astype(jnp.bfloat16)
         b = jnp.where(mine, left_lo, 0.0).astype(jnp.bfloat16)
         wide = lax.dot_general(a, both, nn, preferred_element_type=jnp.float32)
         gram = wide[:, :F] + (
             wide[:, F:] + lax.dot_general(b, hi, nn, preferred_element_type=jnp.float32)
         )
+        tile = jnp.where(sub < 6, total[8 * y : 8 * y + 8], count)
         for x in range(NX):
+            to = NEAR.index(x * NY + y)
             for i in range(OWN):
                 at = (x * OWN + i) * 8
-                out_ref[NEAR.index(x * NY + y), i * 16 + half * 8 : i * 16 + half * 8 + 8, :] = gram[at : at + 8]
+                out_ref[to, i * 8 : i * 8 + 8, :] = gram[at : at + 8]
+            out_ref[to, 48:56, :] = tile
 
 
 def relay_kernel(in_ref, out_ref):
-    y, c, x = lax.axis_index(Y), lax.axis_index(C), lax.axis_index(X)
+    y, z, c, x = (lax.axis_index(axis) for axis in ALL)
     total = jnp.sum(in_ref[...], axis=0)
-    sums, counts = total[96:104], total[102:103]
-    z = lax.broadcasted_iota(jnp.int32, (NZ, 1), 0)
-    lane = lax.broadcasted_iota(jnp.int32, (NZ, F), 1)
-    line = 48 * z + 24 * c + 6 * x
+    sums, counts = total[48:56], total[54:55]
+    q = lax.broadcasted_iota(jnp.int32, (8, 1), 0)
+    lane = lax.broadcasted_iota(jnp.int32, (8, F), 1)
+    line = 96 * q + 48 * (z & 1) + 24 * c + 6 * x
     head, tail = line >> 7, (line + 5) >> 7
 
     def pick(which):
-        out = jnp.zeros((NZ, F), jnp.float32)
+        out = jnp.zeros((8, F), jnp.float32)
         for j in range(6):
             out = jnp.where(which == j, sums[j : j + 1], out)
         return out
@@ -111,11 +110,11 @@
         return jnp.sum(jnp.where(lane == which + 6 * y, counts, 0.0), axis=1, keepdims=True)
 
     def put(i, part):
-        out_ref[0 : NZ - Z0, i, :] = part[Z0:]
-        out_ref[NZ - Z0 :, i, :] = part[:Z0]
+        out_ref[0 : 8 - Z0, i, :] = part[Z0:]
+        out_ref[8 - Z0 :, i, :] = part[:Z0]
 
     for i in range(OWN):
-        part = total[16 * i : 16 * i + 16]
+        part = total[8 * i : 8 * i + 8]
         if i == 1:
             part = jnp.where(lane == (line & 127), number(head), part)
         if i == 5:
@@ -163,7 +162,7 @@
         compiler_params=PARAMS,
         name="pack",
     )(*(pltpu.with_memory_space_constraint(v, pltpu.HBM) for v in (owner, features, key_ids.reshape(2, F))))
-    pair = lax.all_gather(packed, C, tiled=True)
+    pair = lax.all_gather(packed, (Z, C), axis_index_groups=PAIRS, tiled=True)
     partial = pl.pallas_call(
         gram_kernel,
         out_shape=jax.ShapeDtypeStruct((NY * NX, MSG, F), jnp.float32),
@@ -175,13 +174,13 @@
     near = lax.all_to_all(partial, (X, Y), 0, 0, axis_index_groups=[NEAR], tiled=True)
     relayed = pl.pallas_call(
         relay_kernel,
-        out_shape=jax.ShapeDtypeStruct((NZ, 8, F), jnp.float32),
+        out_shape=jax.ShapeDtypeStruct((8, 8, F), jnp.float32),
         in_specs=[VMEM],
         out_specs=VMEM,
         compiler_params=PARAMS,
         name="relay",
     )(near)
-    far = lax.all_to_all(relayed, Z, 0, 0, axis_index_groups=[FAR], tiled=True)
+    far = lax.all_to_all(relayed, Z, 0, 0, axis_index_groups=FAR, tiled=True)
     return pl.pallas_call(
         final_kernel,
         out_shape=jax.ShapeDtypeStruct((OWN, F), jnp.float32),

time: 46.5 us -> 45.8 us (0.985)
  blocking collectives: 42.7 us -> 42 us
    all_gather x1, blocking collectives: 2 us -> 7.69 us  [local(): pair = lax.all_gather(packed, (Z, C), axis_index_groups=PAIRS, tiled=True)]
    all_to_all x1, blocking collectives: 22.1 us -> 16.9 us  [local(): lax.all_to_all(partial, (X, Y), 0, 0, axis_index_groups=[NEAR], tiled=True)]
    all_to_all x1, blocking collectives: 18.6 us -> 17.4 us  [local(): far = lax.all_to_all(relayed, Z, 0, 0, axis_index_groups=FAR, tiled=True)]
where the time goes in v3:
time: 45.8 us; the launch traced here: 45.1 us
  blocking collectives  42 us (92%)
  Pallas kernels  3.08 us (7%)
    all_to_all x1, blocking collectives, local(): far = lax.all_to_all(relayed, Z, 0, 0, axis_index_groups=FAR, tiled=True)  17.4 us
    all_to_all x1, blocking collectives, local(): lax.all_to_all(partial, (X, Y), 0, 0, axis_index_groups=[NEAR], tiled=True)  16.9 us
    all_gather x1, blocking collectives, local(): pair = lax.all_gather(packed, (Z, C), axis_index_groups=PAIRS, tiled=True)  7.69 us
    pallas_call x1, Pallas kernels, local(): pl.pallas_call(gram_kernel, out_shape=jax.ShapeDtypeStruct((NY * NX, MSG,...  1.34 us
    pallas_call x1, Pallas kernels, local(): pl.pallas_call(pack_kernel, out_shape=jax.ShapeDtypeStruct((PACK, F), jnp...  0.95 us

profile of v3, /device:TPU:24, one launch (start us, length us, event | category | flops | bytes accessed | tf_op | source)
XLA Modules:
  0.0 45.1 jit_solution(4611497821542695378)
XLA Ops:
  0.0 0.9 %pack.1 = f32[264,128]{1,0:T(8,128)S(1)} custom-call(s32[24]{0:T(128)} %owner_ref.1, f32[256,128]{1,0:T(8,128)} %features_ref.1, s32[2,128]{1,0:T(2,128)} %bitcast.1), custom_call_target="tpu_custom_call" | custom-call | tf_op jit(solution)/shard_map/pack/pallas_call | solution.py:152
  1.0 7.7 %all_gather.3.rows_ref = f32[1056,128]{1,0:T(8,128)S(1)} all-gather(f32[264,128]{1,0:T(8,128)S(1)} %pack.1), channel_id=1, replica_groups={{0,4,8,12},{16,20,24,28},{32,36,40,44},{48,52,56,60},{64,68,72,76},{80,..., dimensions={0}, use_global_device_ids=true | all-gather | bytes 675840 | tf_op jit(solution)/shard_map/all_gather | solution.py:165
  8.6 1.3 %gram.1 = f32[16,56,128]{2,1,0:T(8,128)S(1)} custom-call(f32[1056,128]{1,0:T(8,128)S(1)} %all_gather.3.rows_ref), custom_call_target="tpu_custom_call" | custom-call | tf_op jit(solution)/shard_map/gram/pallas_call | solution.py:166
  10.0 16.9 %all_to_all.10.in_ref = f32[16,56,128]{2,1,0:T(8,128)S(1)} all-to-all(f32[16,56,128]{2,1,0:T(8,128)S(1)} %gram.1), channel_id=1, replica_groups={{258,386,2,130,259,387,3,131,256,384,0,128,257,385,1,129},{262,390,6,13..., dimensions={0} | all-to-all | bytes 917504 | tf_op jit(solution)/shard_map/all_to_all | solution.py:174
  26.9 0.1 relay.1
  27.0 17.4 %all_to_all.11.in_ref = f32[8,8,128]{2,1,0:T(8,128)S(1)} all-to-all(f32[8,8,128]{2,1,0:T(8,128)S(1)} %relay.1), channel_id=1, replica_groups={{80,96,112,0,16,32,48,64},{88,104,120,8,24,40,56,72},{81,97,113,1,17,33..., dimensions={0} | all-to-all | bytes 65536 | tf_op jit(solution)/shard_map/all_to_all | solution.py:183
  44.4 0.7 %finish.1 = f32[6,128]{1,0:T(8,128)} custom-call(f32[8,8,128]{2,1,0:T(8,128)S(1)} %all_to_all.11.in_ref), custom_call_target="tpu_custom_call" | custom-call | tf_op jit(solution)/shard_map/finish/pallas_call | solution.py:184

commit v4 on v3

--- a/solution.py
+++ b/solution.py
@@ -66,33 +66,39 @@
 
     index = lax.broadcasted_iota(jnp.int32, (32, 1), 0)
     wanted = jnp.where((index & 7) < 6, 6 * (index >> 3) + (index & 7), -1).astype(jnp.float32)
-    onehot = (slot == wanted).astype(jnp.float32).astype(jnp.bfloat16)
-    total = lax.dot_general(onehot, both, nn, preferred_element_type=jnp.float32)
-    total = total[:, :F] + total[:, F:]
-    label = lax.broadcasted_iota(jnp.int32, (F, 1), 0).astype(jnp.float32)
-    every = (slot == label).astype(jnp.float32).astype(jnp.bfloat16)
-    ones = jnp.ones((16, slot.shape[1]), jnp.bfloat16)
-    count = lax.dot_general(ones, every, nt, preferred_element_type=jnp.float32)[0:8]
+    onehot = (slot == wanted).astype(jnp.float32)
+    count = jnp.sum(onehot, axis=1, keepdims=True)
+
+    masks = [relative == float(6 * y) for y in range(NY)]
+    a = jnp.concatenate(
+        [jnp.where(mine, left_hi, 0.0).astype(jnp.bfloat16) for mine in masks]
+        + [onehot.astype(jnp.bfloat16)],
+        axis=0,
+    )
+    b = jnp.concatenate(
+        [jnp.where(mine, left_lo, 0.0).astype(jnp.bfloat16) for mine in masks], axis=0
+    )
+    wide = lax.dot_general(a, both, nn, preferred_element_type=jnp.float32)
+    narrow = lax.dot_general(b, hi, nn, preferred_element_type=jnp.float32)
+    gram = wide[: NY * m, :F] + (wide[: NY * m, F:] + narrow)
+    total = wide[NY * m :, :F] + wide[NY * m :, F:]
     sub = lax.broadcasted_iota(jnp.int32, (8, F), 0)
+    lane = lax.broadcasted_iota(jnp.int32, (8, F), 1)
     for y in range(NY):
-        mine = relative == float(6 * y)
-        a = jnp.where(mine, left_hi, 0.0).astype(jnp.bfloat16)
-        b = jnp.where(mine, left_lo, 0.0).astype(jnp.bfloat16)
-        wide = lax.dot_general(a, both, nn, preferred_element_type=jnp.float32)
-        gram = wide[:, :F] + (
-            wide[:, F:] + lax.dot_general(b, hi, nn, preferred_element_type=jnp.float32)
+        own = jnp.sum(
+            jnp.where(lane == sub, count[8 * y : 8 * y + 8], 0.0), axis=0, keepdims=True
         )
-        tile = jnp.where(sub < 6, total[8 * y : 8 * y + 8], count)
+        tile = jnp.where(sub < 6, total[8 * y : 8 * y + 8], own)
         for x in range(NX):
             to = NEAR.index(x * NY + y)
             for i in range(OWN):
-                at = (x * OWN + i) * 8
+                at = y * m + (x * OWN + i) * 8
                 out_ref[to, i * 8 : i * 8 + 8, :] = gram[at : at + 8]
             out_ref[to, 48:56, :] = tile
 
 
 def relay_kernel(in_ref, out_ref):
-    y, z, c, x = (lax.axis_index(axis) for axis in ALL)
+    z, c, x = lax.axis_index(Z), lax.axis_index(C), lax.axis_index(X)
     total = jnp.sum(in_ref[...], axis=0)
     sums, counts = total[48:56], total[54:55]
     q = lax.broadcasted_iota(jnp.int32, (8, 1), 0)
@@ -107,7 +113,7 @@
         return out
 
     def number(which):
-        return jnp.sum(jnp.where(lane == which + 6 * y, counts, 0.0), axis=1, keepdims=True)
+        return jnp.sum(jnp.where(lane == which, counts, 0.0), axis=1, keepdims=True)
 
     def put(i, part):
         out_ref[0 : 8 - Z0, i, :] = part[Z0:]

time: 45.8 us -> 45.7 us (level)
  no operation moved by 1% of the time
where the time goes in v4:
time: 45.7 us; the launch traced here: 45 us
  blocking collectives  42 us (92%)
  Pallas kernels  2.97 us (6%)
    all_to_all x1, blocking collectives, local(): far = lax.all_to_all(relayed, Z, 0, 0, axis_index_groups=FAR, tiled=True)  17.4 us
    all_to_all x1, blocking collectives, local(): lax.all_to_all(partial, (X, Y), 0, 0, axis_index_groups=[NEAR], tiled=True)  16.9 us
    all_gather x1, blocking collectives, local(): pair = lax.all_gather(packed, (Z, C), axis_index_groups=PAIRS, tiled=True)  7.69 us
    pallas_call x1, Pallas kernels, local(): pl.pallas_call(gram_kernel, out_shape=jax.ShapeDtypeStruct((NY * NX, MSG,...  1.23 us
    pallas_call x1, Pallas kernels, local(): pl.pallas_call(pack_kernel, out_shape=jax.ShapeDtypeStruct((PACK, F), jnp...  0.95 us

profile of v4, /device:TPU:24, one launch (start us, length us, event | category | flops | bytes accessed | tf_op | source)
XLA Modules:
  0.0 45.0 jit_solution(2292703134461260589)
XLA Ops:
  0.0 0.9 %pack.1 = f32[264,128]{1,0:T(8,128)S(1)} custom-call(s32[24]{0:T(128)} %owner_ref.1, f32[256,128]{1,0:T(8,128)} %features_ref.1, s32[2,128]{1,0:T(2,128)} %bitcast.1), custom_call_target="tpu_custom_call" | custom-call | tf_op jit(solution)/shard_map/pack/pallas_call | solution.py:158
  1.0 7.7 %all_gather.3.rows_ref = f32[1056,128]{1,0:T(8,128)S(1)} all-gather(f32[264,128]{1,0:T(8,128)S(1)} %pack.1), channel_id=1, replica_groups={{0,4,8,12},{16,20,24,28},{32,36,40,44},{48,52,56,60},{64,68,72,76},{80,..., dimensions={0}, use_global_device_ids=true | all-gather | bytes 675840 | tf_op jit(solution)/shard_map/all_gather | solution.py:171
  8.6 1.2 %gram.1 = f32[16,56,128]{2,1,0:T(8,128)S(1)} custom-call(f32[1056,128]{1,0:T(8,128)S(1)} %all_gather.3.rows_ref), custom_call_target="tpu_custom_call" | custom-call | tf_op jit(solution)/shard_map/gram/pallas_call | solution.py:172
  9.9 16.9 %all_to_all.10.in_ref = f32[16,56,128]{2,1,0:T(8,128)S(1)} all-to-all(f32[16,56,128]{2,1,0:T(8,128)S(1)} %gram.1), channel_id=1, replica_groups={{258,386,2,130,259,387,3,131,256,384,0,128,257,385,1,129},{262,390,6,13..., dimensions={0} | all-to-all | bytes 917504 | tf_op jit(solution)/shard_map/all_to_all | solution.py:180
  26.8 0.1 relay.1
  26.9 17.4 %all_to_all.11.in_ref = f32[8,8,128]{2,1,0:T(8,128)S(1)} all-to-all(f32[8,8,128]{2,1,0:T(8,128)S(1)} %relay.1), channel_id=1, replica_groups={{80,96,112,0,16,32,48,64},{88,104,120,8,24,40,56,72},{81,97,113,1,17,33..., dimensions={0} | all-to-all | bytes 65536 | tf_op jit(solution)/shard_map/all_to_all | solution.py:189
  44.3 0.7 %finish.1 = f32[6,128]{1,0:T(8,128)} custom-call(f32[8,8,128]{2,1,0:T(8,128)S(1)} %all_to_all.11.in_ref), custom_call_target="tpu_custom_call" | custom-call | tf_op jit(solution)/shard_map/finish/pallas_call | solution.py:190

commit v5 on v4

--- a/solution.py
+++ b/solution.py
@@ -79,8 +79,8 @@
         [jnp.where(mine, left_lo, 0.0).astype(jnp.bfloat16) for mine in masks], axis=0
     )
     wide = lax.dot_general(a, both, nn, preferred_element_type=jnp.float32)
-    narrow = lax.dot_general(b, hi, nn, preferred_element_type=jnp.float32)
-    gram = wide[: NY * m, :F] + (wide[: NY * m, F:] + narrow)
+    fine = lax.dot_general(b, both, nn, preferred_element_type=jnp.float32)
+    gram = wide[: NY * m, :F] + (wide[: NY * m, F:] + (fine[:, :F] + fine[:, F:]))
     total = wide[NY * m :, :F] + wide[NY * m :, F:]
     sub = lax.broadcasted_iota(jnp.int32, (8, F), 0)
     lane = lax.broadcasted_iota(jnp.int32, (8, F), 1)

time: 45.7 us -> 45.7 us (level)
  no operation moved by 1% of the time
where the time goes in v5:
time: 45.7 us; the launch traced here: 45 us
  blocking collectives  42 us (92%)
  Pallas kernels  2.97 us (6%)
    all_to_all x1, blocking collectives, local(): far = lax.all_to_all(relayed, Z, 0, 0, axis_index_groups=FAR, tiled=True)  17.4 us
    all_to_all x1, blocking collectives, local(): lax.all_to_all(partial, (X, Y), 0, 0, axis_index_groups=[NEAR], tiled=True)  16.9 us
    all_gather x1, blocking collectives, local(): pair = lax.all_gather(packed, (Z, C), axis_index_groups=PAIRS, tiled=True)  7.69 us
    pallas_call x1, Pallas kernels, local(): pl.pallas_call(gram_kernel, out_shape=jax.ShapeDtypeStruct((NY * NX, MSG,...  1.23 us
    pallas_call x1, Pallas kernels, local(): pl.pallas_call(pack_kernel, out_shape=jax.ShapeDtypeStruct((PACK, F), jnp...  0.95 us

profile of v5, /device:TPU:24, one launch (start us, length us, event | category | flops | bytes accessed | tf_op | source)
XLA Modules:
  0.0 45.0 jit_solution(1282994576897315693)
XLA Ops:
  0.0 0.9 %pack.1 = f32[264,128]{1,0:T(8,128)S(1)} custom-call(s32[24]{0:T(128)} %owner_ref.1, f32[256,128]{1,0:T(8,128)} %features_ref.1, s32[2,128]{1,0:T(2,128)} %bitcast.1), custom_call_target="tpu_custom_call" | custom-call | tf_op jit(solution)/shard_map/pack/pallas_call | solution.py:158
  1.0 7.7 %all_gather.3.rows_ref = f32[1056,128]{1,0:T(8,128)S(1)} all-gather(f32[264,128]{1,0:T(8,128)S(1)} %pack.1), channel_id=1, replica_groups={{0,4,8,12},{16,20,24,28},{32,36,40,44},{48,52,56,60},{64,68,72,76},{80,..., dimensions={0}, use_global_device_ids=true | all-gather | bytes 675840 | tf_op jit(solution)/shard_map/all_gather | solution.py:171
  8.6 1.2 %gram.1 = f32[16,56,128]{2,1,0:T(8,128)S(1)} custom-call(f32[1056,128]{1,0:T(8,128)S(1)} %all_gather.3.rows_ref), custom_call_target="tpu_custom_call" | custom-call | tf_op jit(solution)/shard_map/gram/pallas_call | solution.py:172
  9.9 16.9 %all_to_all.10.in_ref = f32[16,56,128]{2,1,0:T(8,128)S(1)} all-to-all(f32[16,56,128]{2,1,0:T(8,128)S(1)} %gram.1), channel_id=1, replica_groups={{258,386,2,130,259,387,3,131,256,384,0,128,257,385,1,129},{262,390,6,13..., dimensions={0} | all-to-all | bytes 917504 | tf_op jit(solution)/shard_map/all_to_all | solution.py:180
  26.8 0.1 relay.1
  26.9 17.4 %all_to_all.11.in_ref = f32[8,8,128]{2,1,0:T(8,128)S(1)} all-to-all(f32[8,8,128]{2,1,0:T(8,128)S(1)} %relay.1), channel_id=1, replica_groups={{80,96,112,0,16,32,48,64},{88,104,120,8,24,40,56,72},{81,97,113,1,17,33..., dimensions={0} | all-to-all | bytes 65536 | tf_op jit(solution)/shard_map/all_to_all | solution.py:189
  44.3 0.7 %finish.1 = f32[6,128]{1,0:T(8,128)} custom-call(f32[8,8,128]{2,1,0:T(8,128)S(1)} %all_to_all.11.in_ref), custom_call_target="tpu_custom_call" | custom-call | tf_op jit(solution)/shard_map/finish/pallas_call | solution.py:190

commit v6 on v5

--- a/solution.py
+++ b/solution.py
@@ -13,6 +13,7 @@
 NY, NZ, NX = 4, 16, 4
 OWN = 6
 PACK = 264
+PARTS = 4
 MSG = 56
 VMEM = pl.BlockSpec(memory_space=pltpu.VMEM)
 HBM = pl.BlockSpec(memory_space=pltpu.HBM)
@@ -28,8 +29,13 @@
     copies = [
         pltpu.make_async_copy(owner_ref, owner_buf, sems.at[0]),
         pltpu.make_async_copy(keys_ref, keys_buf, sems.at[1]),
-        pltpu.make_async_copy(features_ref, out_ref.at[0:rows, :], sems.at[2]),
     ]
+    step = rows // PARTS
+    for part in range(PARTS):
+        lines = pl.ds(part * step, step)
+        copies.append(
+            pltpu.make_async_copy(features_ref.at[lines, :], out_ref.at[lines, :], sems.at[2 + part])
+        )
     for copy in copies:
         copy.start()
     copies[0].wait()
@@ -39,7 +45,8 @@
     for key in range(KEYS):
         slot = jnp.where(keys == key, owner_buf[key].astype(jnp.float32), slot)
     out_ref[rows:, :] = jnp.concatenate([slot, jnp.zeros((6, F), jnp.float32)], axis=0)
-    copies[2].wait()
+    for copy in copies[2:]:
+        copy.wait()
 
 
 def gram_kernel(rows_ref, out_ref):
@@ -53,35 +60,38 @@
     lo = (feats - hi.astype(jnp.float32)).astype(jnp.bfloat16)
     both = jnp.concatenate([hi, lo], axis=1)
 
-    m = NX * OWN * 8
+    m = NX * OWN * 4
     index = lax.broadcasted_iota(jnp.int32, (m, 1), 0)
-    line = 96 * (index & 7) + 48 * (z & 1) + 24 * c + (index >> 3)
+    line = 96 * (index & 3) + 48 * (z & 1) + 24 * c + (index >> 2)
     lane = lax.broadcasted_iota(jnp.int32, (m, F), 1)
     select = (lane == (line & 127)).astype(jnp.float32).astype(jnp.bfloat16)
     nt = (((1,), (1,)), ((), ()))
     nn = (((1,), (0,)), ((), ()))
     left_hi = lax.dot_general(select, hi, nt, preferred_element_type=jnp.float32)
+    left_hi = left_hi.astype(jnp.bfloat16)
     left_lo = lax.dot_general(select, lo, nt, preferred_element_type=jnp.float32)
-    relative = slot - (line >> 7).astype(jnp.float32)
+    left_lo = left_lo.astype(jnp.bfloat16)
+    relative = (slot - (line >> 7).astype(jnp.float32)).astype(jnp.bfloat16)
 
     index = lax.broadcasted_iota(jnp.int32, (32, 1), 0)
     wanted = jnp.where((index & 7) < 6, 6 * (index >> 3) + (index & 7), -1).astype(jnp.float32)
     onehot = (slot == wanted).astype(jnp.float32)
     count = jnp.sum(onehot, axis=1, keepdims=True)
 
-    masks = [relative == float(6 * y) for y in range(NY)]
+    zero = jnp.zeros((), jnp.bfloat16)
+    masks = [relative == jnp.bfloat16(3 * group) for group in range(2 * NY)]
     a = jnp.concatenate(
-        [jnp.where(mine, left_hi, 0.0).astype(jnp.bfloat16) for mine in masks]
+        [jnp.where(mine, left_hi, zero) for mine in masks]
         + [onehot.astype(jnp.bfloat16)],
         axis=0,
     )
     b = jnp.concatenate(
-        [jnp.where(mine, left_lo, 0.0).astype(jnp.bfloat16) for mine in masks], axis=0
+        [jnp.where(mine, left_lo, zero) for mine in masks], axis=0
     )
     wide = lax.dot_general(a, both, nn, preferred_element_type=jnp.float32)
     fine = lax.dot_general(b, both, nn, preferred_element_type=jnp.float32)
-    gram = wide[: NY * m, :F] + (wide[: NY * m, F:] + (fine[:, :F] + fine[:, F:]))
-    total = wide[NY * m :, :F] + wide[NY * m :, F:]
+    gram = wide[: 2 * NY * m, :F] + (wide[: 2 * NY * m, F:] + (fine[:, :F] + fine[:, F:]))
+    total = wide[2 * NY * m :, :F] + wide[2 * NY * m :, F:]
     sub = lax.broadcasted_iota(jnp.int32, (8, F), 0)
     lane = lax.broadcasted_iota(jnp.int32, (8, F), 1)
     for y in range(NY):
@@ -91,9 +101,9 @@
         tile = jnp.where(sub < 6, total[8 * y : 8 * y + 8], own)
         for x in range(NX):
             to = NEAR.index(x * NY + y)
-            for i in range(OWN):
-                at = y * m + (x * OWN + i) * 8
-                out_ref[to, i * 8 : i * 8 + 8, :] = gram[at : at + 8]
+            for half in range(2):
+                at = (2 * y + half) * m + x * 24
+                out_ref[to, half * 24 : half * 24 + 24, :] = gram[at : at + 24]
             out_ref[to, 48:56, :] = tile
 
 
@@ -120,7 +130,7 @@
         out_ref[8 - Z0 :, i, :] = part[:Z0]
 
     for i in range(OWN):
-        part = total[8 * i : 8 * i + 8]
+        part = jnp.concatenate([total[4 * i : 4 * i + 4], total[24 + 4 * i : 28 + 4 * i]], axis=0)
         if i == 1:
             part = jnp.where(lane == (line & 127), number(head), part)
         if i == 5:
@@ -163,7 +173,7 @@
         scratch_shapes=[
             pltpu.SMEM((KEYS,), jnp.int32),
             pltpu.VMEM((2, F), jnp.int32),
-            pltpu.SemaphoreType.DMA((3,)),
+            pltpu.SemaphoreType.DMA((2 + PARTS,)),
         ],
         compiler_params=PARAMS,
         name="pack",

time: 45.7 us -> 45.7 us (level)
  no operation moved by 1% of the time
where the time goes in v6:
time: 45.7 us; the launch traced here: 44.8 us
  blocking collectives  42 us (92%)
  Pallas kernels  2.84 us (6%)
    all_to_all x1, blocking collectives, local(): far = lax.all_to_all(relayed, Z, 0, 0, axis_index_groups=FAR, tiled=True)  17.4 us
    all_to_all x1, blocking collectives, local(): lax.all_to_all(partial, (X, Y), 0, 0, axis_index_groups=[NEAR], tiled=True)  16.9 us
    all_gather x1, blocking collectives, local(): pair = lax.all_gather(packed, (Z, C), axis_index_groups=PAIRS, tiled=True)  7.69 us
    pallas_call x1, Pallas kernels, local(): pl.pallas_call(gram_kernel, out_shape=jax.ShapeDtypeStruct((NY * NX, MSG,...  1.18 us

profile of v6, /device:TPU:24, one launch (start us, length us, event | category | flops | bytes accessed | tf_op | source)
XLA Modules:
  0.0 44.8 jit_solution(4485704386936320514)
XLA Ops:
  0.0 0.9 %pack.1 = f32[264,128]{1,0:T(8,128)S(1)} custom-call(s32[24]{0:T(128)} %owner_ref.1, f32[256,128]{1,0:T(8,128)} %features_ref.1, s32[2,128]{1,0:T(2,128)} %bitcast.1), custom_call_target="tpu_custom_call" | custom-call | tf_op jit(solution)/shard_map/pack/pallas_call | solution.py:168
  0.9 7.7 %all_gather.3.rows_ref = f32[1056,128]{1,0:T(8,128)S(1)} all-gather(f32[264,128]{1,0:T(8,128)S(1)} %pack.1), channel_id=1, replica_groups={{0,4,8,12},{16,20,24,28},{32,36,40,44},{48,52,56,60},{64,68,72,76},{80,..., dimensions={0}, use_global_device_ids=true | all-gather | bytes 675840 | tf_op jit(solution)/shard_map/all_gather | solution.py:181
  8.6 1.2 %gram.1 = f32[16,56,128]{2,1,0:T(8,128)S(1)} custom-call(f32[1056,128]{1,0:T(8,128)S(1)} %all_gather.3.rows_ref), custom_call_target="tpu_custom_call" | custom-call | tf_op jit(solution)/shard_map/gram/pallas_call | solution.py:182
  9.8 16.9 %all_to_all.10.in_ref = f32[16,56,128]{2,1,0:T(8,128)S(1)} all-to-all(f32[16,56,128]{2,1,0:T(8,128)S(1)} %gram.1), channel_id=1, replica_groups={{258,386,2,130,259,387,3,131,256,384,0,128,257,385,1,129},{262,390,6,13..., dimensions={0} | all-to-all | bytes 917504 | tf_op jit(solution)/shard_map/all_to_all | solution.py:190
  26.7 0.1 relay.1
  26.8 17.4 %all_to_all.11.in_ref = f32[8,8,128]{2,1,0:T(8,128)S(1)} all-to-all(f32[8,8,128]{2,1,0:T(8,128)S(1)} %relay.1), channel_id=1, replica_groups={{80,96,112,0,16,32,48,64},{88,104,120,8,24,40,56,72},{81,97,113,1,17,33..., dimensions={0} | all-to-all | bytes 65536 | tf_op jit(solution)/shard_map/all_to_all | solution.py:199
  44.1 0.7 %finish.1 = f32[6,128]{1,0:T(8,128)} custom-call(f32[8,8,128]{2,1,0:T(8,128)S(1)} %all_to_all.11.in_ref), custom_call_target="tpu_custom_call" | custom-call | tf_op jit(solution)/shard_map/finish/pallas_call | solution.py:200

commit v7 on v6

--- a/solution.py
+++ b/solution.py
@@ -17,7 +17,7 @@
 MSG = 56
 VMEM = pl.BlockSpec(memory_space=pltpu.VMEM)
 HBM = pl.BlockSpec(memory_space=pltpu.HBM)
-Y0, Z0, X0 = 2, 5, 2
+Y0, Z0, X0 = 2, 4, 2
 NEAR = [(i + X0) % NX * NY + (j + Y0) % NY for i in range(NX) for j in range(NY)]
 FAR = [[(2 * (k + Z0) + odd) % NZ for k in range(8)] for odd in range(2)]
 PAIRS = [[4 * k + j for j in range(4)] for k in range(8)]

time: 45.7 us -> 45.7 us (level)
  no operation moved by 1% of the time
where the time goes in v7:
time: 45.7 us; the launch traced here: 44.9 us
  blocking collectives  42 us (92%)
  Pallas kernels  2.84 us (6%)
    all_to_all x1, blocking collectives, local(): far = lax.all_to_all(relayed, Z, 0, 0, axis_index_groups=FAR, tiled=True)  17.4 us
    all_to_all x1, blocking collectives, local(): lax.all_to_all(partial, (X, Y), 0, 0, axis_index_groups=[NEAR], tiled=True)  16.9 us
    all_gather x1, blocking collectives, local(): pair = lax.all_gather(packed, (Z, C), axis_index_groups=PAIRS, tiled=True)  7.69 us
    pallas_call x1, Pallas kernels, local(): pl.pallas_call(gram_kernel, out_shape=jax.ShapeDtypeStruct((NY * NX, MSG,...  1.18 us

profile of v7, /device:TPU:24, one launch (start us, length us, event | category | flops | bytes accessed | tf_op | source)
XLA Modules:
  0.0 44.9 jit_solution(10957044925789420134)
XLA Ops:
  0.0 0.9 %pack.1 = f32[264,128]{1,0:T(8,128)S(1)} custom-call(s32[24]{0:T(128)} %owner_ref.1, f32[256,128]{1,0:T(8,128)} %features_ref.1, s32[2,128]{1,0:T(2,128)} %bitcast.1), custom_call_target="tpu_custom_call" | custom-call | tf_op jit(solution)/shard_map/pack/pallas_call | solution.py:168
  0.9 7.7 %all_gather.3.rows_ref = f32[1056,128]{1,0:T(8,128)S(1)} all-gather(f32[264,128]{1,0:T(8,128)S(1)} %pack.1), channel_id=1, replica_groups={{0,4,8,12},{16,20,24,28},{32,36,40,44},{48,52,56,60},{64,68,72,76},{80,..., dimensions={0}, use_global_device_ids=true | all-gather | bytes 675840 | tf_op jit(solution)/shard_map/all_gather | solution.py:181
  8.6 1.2 %gram.1 = f32[16,56,128]{2,1,0:T(8,128)S(1)} custom-call(f32[1056,128]{1,0:T(8,128)S(1)} %all_gather.3.rows_ref), custom_call_target="tpu_custom_call" | custom-call | tf_op jit(solution)/shard_map/gram/pallas_call | solution.py:182
  9.8 16.9 %all_to_all.10.in_ref = f32[16,56,128]{2,1,0:T(8,128)S(1)} all-to-all(f32[16,56,128]{2,1,0:T(8,128)S(1)} %gram.1), channel_id=1, replica_groups={{258,386,2,130,259,387,3,131,256,384,0,128,257,385,1,129},{262,390,6,13..., dimensions={0} | all-to-all | bytes 917504 | tf_op jit(solution)/shard_map/all_to_all | solution.py:190
  26.7 0.1 relay.1
  26.8 17.4 %all_to_all.11.in_ref = f32[8,8,128]{2,1,0:T(8,128)S(1)} all-to-all(f32[8,8,128]{2,1,0:T(8,128)S(1)} %relay.1), channel_id=1, replica_groups={{64,80,96,112,0,16,32,48},{72,88,104,120,8,24,40,56},{65,81,97,113,1,17..., dimensions={0} | all-to-all | bytes 65536 | tf_op jit(solution)/shard_map/all_to_all | solution.py:199
  44.2 0.7 %finish.1 = f32[6,128]{1,0:T(8,128)} custom-call(f32[8,8,128]{2,1,0:T(8,128)S(1)} %all_to_all.11.in_ref), custom_call_target="tpu_custom_call" | custom-call | tf_op jit(solution)/shard_map/finish/pallas_call | solution.py:200

commit v8 on v5

--- a/solution.py
+++ b/solution.py
@@ -13,6 +13,7 @@
 NY, NZ, NX = 4, 16, 4
 OWN = 6
 PACK = 264
+PARTS = 4
 MSG = 56
 VMEM = pl.BlockSpec(memory_space=pltpu.VMEM)
 HBM = pl.BlockSpec(memory_space=pltpu.HBM)
@@ -28,8 +29,13 @@
     copies = [
         pltpu.make_async_copy(owner_ref, owner_buf, sems.at[0]),
         pltpu.make_async_copy(keys_ref, keys_buf, sems.at[1]),
-        pltpu.make_async_copy(features_ref, out_ref.at[0:rows, :], sems.at[2]),
     ]
+    step = rows // PARTS
+    for part in range(PARTS):
+        lines = pl.ds(part * step, step)
+        copies.append(
+            pltpu.make_async_copy(features_ref.at[lines, :], out_ref.at[lines, :], sems.at[2 + part])
+        )
     for copy in copies:
         copy.start()
     copies[0].wait()
@@ -39,7 +45,8 @@
     for key in range(KEYS):
         slot = jnp.where(keys == key, owner_buf[key].astype(jnp.float32), slot)
     out_ref[rows:, :] = jnp.concatenate([slot, jnp.zeros((6, F), jnp.float32)], axis=0)
-    copies[2].wait()
+    for copy in copies[2:]:
+        copy.wait()
 
 
 def gram_kernel(rows_ref, out_ref):
@@ -163,7 +170,7 @@
         scratch_shapes=[
             pltpu.SMEM((KEYS,), jnp.int32),
             pltpu.VMEM((2, F), jnp.int32),
-            pltpu.SemaphoreType.DMA((3,)),
+            pltpu.SemaphoreType.DMA((2 + PARTS,)),
         ],
         compiler_params=PARAMS,
         name="pack",

time: 45.7 us -> 45.7 us (level)
  no operation moved by 1% of the time
where the time goes in v8:
time: 45.7 us; the launch traced here: 44.9 us
  blocking collectives  42 us (92%)
  Pallas kernels  2.9 us (6%)
    all_to_all x1, blocking collectives, local(): far = lax.all_to_all(relayed, Z, 0, 0, axis_index_groups=FAR, tiled=True)  17.4 us
    all_to_all x1, blocking collectives, local(): lax.all_to_all(partial, (X, Y), 0, 0, axis_index_groups=[NEAR], tiled=True)  16.9 us
    all_gather x1, blocking collectives, local(): pair = lax.all_gather(packed, (Z, C), axis_index_groups=PAIRS, tiled=True)  7.69 us
    pallas_call x1, Pallas kernels, local(): pl.pallas_call(gram_kernel, out_shape=jax.ShapeDtypeStruct((NY * NX, MSG,...  1.23 us

profile of v8, /device:TPU:24, one launch (start us, length us, event | category | flops | bytes accessed | tf_op | source)
XLA Modules:
  0.0 44.9 jit_solution(8922300084429021624)
XLA Ops:
  0.0 0.9 %pack.1 = f32[264,128]{1,0:T(8,128)S(1)} custom-call(s32[24]{0:T(128)} %owner_ref.1, f32[256,128]{1,0:T(8,128)} %features_ref.1, s32[2,128]{1,0:T(2,128)} %bitcast.1), custom_call_target="tpu_custom_call" | custom-call | tf_op jit(solution)/shard_map/pack/pallas_call | solution.py:165
  0.9 7.7 %all_gather.3.rows_ref = f32[1056,128]{1,0:T(8,128)S(1)} all-gather(f32[264,128]{1,0:T(8,128)S(1)} %pack.1), channel_id=1, replica_groups={{0,4,8,12},{16,20,24,28},{32,36,40,44},{48,52,56,60},{64,68,72,76},{80,..., dimensions={0}, use_global_device_ids=true | all-gather | bytes 675840 | tf_op jit(solution)/shard_map/all_gather | solution.py:178
  8.6 1.2 %gram.1 = f32[16,56,128]{2,1,0:T(8,128)S(1)} custom-call(f32[1056,128]{1,0:T(8,128)S(1)} %all_gather.3.rows_ref), custom_call_target="tpu_custom_call" | custom-call | tf_op jit(solution)/shard_map/gram/pallas_call | solution.py:179
  9.8 16.9 %all_to_all.10.in_ref = f32[16,56,128]{2,1,0:T(8,128)S(1)} all-to-all(f32[16,56,128]{2,1,0:T(8,128)S(1)} %gram.1), channel_id=1, replica_groups={{258,386,2,130,259,387,3,131,256,384,0,128,257,385,1,129},{262,390,6,13..., dimensions={0} | all-to-all | bytes 917504 | tf_op jit(solution)/shard_map/all_to_all | solution.py:187
  26.8 0.1 relay.1
  26.9 17.4 %all_to_all.11.in_ref = f32[8,8,128]{2,1,0:T(8,128)S(1)} all-to-all(f32[8,8,128]{2,1,0:T(8,128)S(1)} %relay.1), channel_id=1, replica_groups={{80,96,112,0,16,32,48,64},{88,104,120,8,24,40,56,72},{81,97,113,1,17,33..., dimensions={0} | all-to-all | bytes 65536 | tf_op jit(solution)/shard_map/all_to_all | solution.py:196
  44.2 0.7 %finish.1 = f32[6,128]{1,0:T(8,128)} custom-call(f32[8,8,128]{2,1,0:T(8,128)S(1)} %all_to_all.11.in_ref), custom_call_target="tpu_custom_call" | custom-call | tf_op jit(solution)/shard_map/finish/pallas_call | solution.py:197
